TPU v7x, 512 devices: a whole 4x4x16 slice. The times are simulated.
512 devices in a mesh: depth: 8 (over z_hi, core), lat: 64 (over x, z_lo, y).
Axes of the slice: x: 4, y: 4, z: 16 (z_hi: 4, z_lo: 4; z = z_hi * 4 + z_lo), core: 2. Of those that a mesh axis runs over, the one named last changes fastest.
Arguments:
- fields: float32 [6, 384, 64, 512], P(None, 'lat', 'depth'), may hold values from -3 to 3
- material: int32 [384, 64, 512], P('lat', 'depth'), may hold values from 0 to 3
- source_mask: int32 [384, 64, 512], P('lat', 'depth'), may hold values 0 or 1
- eps_table: float32 [4], replicated, may hold values from 1 to 6
- kerr_table: float32 [4], replicated, may hold values from 0.3 to 3
Outputs:
- fields_out: float32 [6, 384, 64, 512], P(None, 'lat', 'depth')
- image: float32 [384, 8, 512], P('lat', None, 'depth')
Inputs may be any that keep to these rules, and one draw needn't show every extreme that they name: material indexes the tables.
All inputs are finite; a program needn't handle non-finite values. No bound on the sum of `source_mask` on one device may be relied on, other than what follows from the above.
Results may differ from a plain program's by a relative error of at most 0.0003.
Values sent between devices are 32-bit elements; how exact they have to be, the bound alone decides.
A program may use at most 64 MiB of HBM per device.

v0:
```python
import math
import jax
import jax.numpy as jnp
from jax import lax
from jax.sharding import PartitionSpec as P

STEPS = 16
COURANT = 0.55
OMEGAS = (0.9, 1.3)
SOURCE_AMP = 1.0
QUARTERS = (3, 5)
HIGHEST = lax.Precision.HIGHEST


def padded_2(block, sides, width):
    for axis, dim in sides:
        count = lax.axis_size(axis)
        forward = [(i, i + 1) for i in range(count - 1)]
        backward = [(target, source) for source, target in forward]
        low = lax.ppermute(
            lax.slice_in_dim(block, block.shape[dim] - width, None, axis=dim), axis, forward
        )
        high = lax.ppermute(lax.slice_in_dim(block, 0, width, axis=dim), axis, backward)
        block = jnp.concatenate([low, block, high], axis=dim)
    return block


def from_root(block, axis, owner):
    block = jnp.where(lax.axis_index(axis) == owner, block, jnp.zeros_like(block))
    return lax.psum(block, axis)


def forward_diff(field, along):
    length = field.shape[along]
    ahead = lax.slice_in_dim(field, 1, length, axis=along)
    ahead = jnp.concatenate(
        [ahead, jnp.zeros_like(lax.slice_in_dim(field, 0, 1, axis=along))], axis=along
    )
    return ahead - field


def backward_diff(field, along):
    length = field.shape[along]
    behind = lax.slice_in_dim(field, 0, length - 1, axis=along)
    behind = jnp.concatenate(
        [jnp.zeros_like(lax.slice_in_dim(field, 0, 1, axis=along)), behind], axis=along
    )
    return field - behind


def drive(moment):
    middle = moment + 0.5
    return SOURCE_AMP * (jnp.sin(OMEGAS[0] * middle) + jnp.sin(OMEGAS[1] * middle))


def yee_step(fields, permittivity, kerr_coef, source_flag, inside, pulse):
    elec_x, elec_y, elec_z = (fields[0], fields[1], fields[2])
    magn_x, magn_y, magn_z = (fields[3], fields[4], fields[5])
    magn_x = (magn_x - COURANT * (forward_diff(elec_z, 2) - forward_diff(elec_y, 1))) * inside
    magn_y = (magn_y - COURANT * (forward_diff(elec_x, 1) - forward_diff(elec_z, 0))) * inside
    magn_z = (magn_z - COURANT * (forward_diff(elec_y, 0) - forward_diff(elec_x, 2))) * inside
    energy = elec_x * elec_x + elec_y * elec_y + elec_z * elec_z
    factor = COURANT / (permittivity + kerr_coef * energy)
    new_x = (
        elec_x
        + factor * (backward_diff(magn_z, 2) - backward_diff(magn_y, 1))
        + source_flag * pulse
    ) * inside
    new_y = (elec_y + factor * (backward_diff(magn_x, 1) - backward_diff(magn_z, 0))) * inside
    new_z = (elec_z + factor * (backward_diff(magn_y, 0) - backward_diff(magn_x, 2))) * inside
    return jnp.stack([new_x, new_y, new_z, magn_x, magn_y, magn_z])


def lookup(material, table):
    result = jnp.zeros(material.shape, jnp.float32)
    for level in range(table.shape[0]):
        result = jnp.where(material == level, table[level], result)
    return result


def accumulate(spectrum, plane, moment):
    later = moment + 1.0
    trig = jnp.stack(
        [jnp.stack([jnp.cos(omega * later), -jnp.sin(omega * later)]) for omega in OMEGAS]
    )
    return spectrum + trig[:, None, :, None, None] * plane[None, :, None, :, :]


def chirp(row_index, col_index, length):
    gap = row_index[:, None] - col_index[None, :]
    squared = gap * gap
    reals, imags = ([], [])
    for quarter in QUARTERS:
        wrapped = quarter * squared % (8 * length)
        phase = wrapped.astype(jnp.float32) * (math.pi / (4.0 * length))
        reals.append(jnp.cos(phase) / math.sqrt(length))
        imags.append(jnp.sin(phase) / math.sqrt(length))
    return (jnp.stack(reals), jnp.stack(imags))


def column_transform(real, imag, y_real, y_imag):
    v_real = jnp.einsum("fcxy,fyk->fcxk", real, y_real, precision=HIGHEST) - jnp.einsum(
        "fcxy,fyk->fcxk", imag, y_imag, precision=HIGHEST
    )
    v_imag = jnp.einsum("fcxy,fyk->fcxk", real, y_imag, precision=HIGHEST) + jnp.einsum(
        "fcxy,fyk->fcxk", imag, y_real, precision=HIGHEST
    )
    return (v_real, v_imag)


def row_transform(x_real, x_imag, v_real, v_imag):
    w_real = jnp.einsum("fix,fcxk->ifck", x_real, v_real, precision=HIGHEST) - jnp.einsum(
        "fix,fcxk->ifck", x_imag, v_imag, precision=HIGHEST
    )
    w_imag = jnp.einsum("fix,fcxk->ifck", x_real, v_imag, precision=HIGHEST) + jnp.einsum(
        "fix,fcxk->ifck", x_imag, v_real, precision=HIGHEST
    )
    return jnp.stack([w_real, w_imag], axis=3)


def local(fields, material, source_mask, eps_table, kerr_table):
    width_x = fields.shape[1]
    depth_z = fields.shape[2]
    span_y = fields.shape[3]
    lat_count = lax.axis_size("lat")
    depth_count = lax.axis_size("depth")
    total_x = width_x * lat_count
    total_z = depth_z * depth_count
    lat_pos = lax.axis_index("lat")
    depth_pos = lax.axis_index("depth")
    coefs = jnp.stack(
        [lookup(material, eps_table), lookup(material, kerr_table), source_mask.astype(jnp.float32)]
    )
    empty_spectrum = jnp.zeros((2, 2, 2, width_x, span_y), jnp.float32)
    rim_width = ((0, 0), (1, 1), (1, 1), (0, 0))
    eps_pad = jnp.pad(coefs[0:1], rim_width, constant_values=1.0)
    rest_pad = jnp.pad(coefs[1:3], rim_width, constant_values=0.0)
    sub = jnp.concatenate([eps_pad, rest_pad], axis=0)
    place_x = lat_pos * width_x - 1 + jnp.arange(width_x + 2 * 1, dtype=jnp.int32)
    place_z = depth_pos * depth_z - 1 + jnp.arange(depth_z + 2 * 1, dtype=jnp.int32)
    valid_x = (place_x >= 0) & (place_x < total_x)
    valid_z = (place_z >= 0) & (place_z < total_z)
    valid = valid_x[:, None] & valid_z[None, :]
    setup_inside = valid.astype(jnp.float32)[:, :, None]
    setup_permittivity = jnp.where(valid[:, :, None], sub[0], 1.0)
    kerr_coef = sub[1]
    source_flag = sub[2]

    def one_step(step, carry):
        state, spectrum = carry
        padded = padded_2(state, (("depth", 2), ("lat", 1)), 1)
        moment = step.astype(jnp.float32)
        padded = yee_step(
            padded, setup_permittivity, kerr_coef, source_flag, setup_inside, drive(moment)
        )
        state = padded[:, 1:-1, 1:-1]
        spectrum = accumulate(spectrum, state[0:2, :, depth_z - 1, :], moment)
        return (state, spectrum)

    state, spectrum = lax.fori_loop(0, STEPS, one_step, (fields, empty_spectrum))
    spectrum = from_root(spectrum, "depth", depth_count - 1)
    col_count = span_y // depth_count
    col_index = depth_pos * col_count + jnp.arange(col_count, dtype=jnp.int32)
    y_real, y_imag = chirp(jnp.arange(span_y, dtype=jnp.int32), col_index, span_y)
    v_real, v_imag = column_transform(spectrum[:, :, 0], spectrum[:, :, 1], y_real, y_imag)
    row_local = lat_pos * width_x + jnp.arange(width_x, dtype=jnp.int32)
    row_index = jnp.arange(width_x * lax.axis_size("lat"), dtype=jnp.int32)
    x_real, x_imag = chirp(row_index, row_local, total_x)
    image = lax.psum_scatter(
        row_transform(x_real, x_imag, v_real, v_imag), "lat", scatter_dimension=0, tiled=True
    )
    return (state, image.reshape(width_x, 8, col_count))


def solution(mesh):
    placed = (
        P(None, "lat", "depth", None),
        P("lat", "depth", None),
        P("lat", "depth", None),
        P(),
        P(),
    )
    return jax.shard_map(
        local,
        mesh=mesh,
        in_specs=placed,
        out_specs=(P(None, "lat", "depth", None), P("lat", None, "depth")),
        check_vma=False,
    )
```

profile of v0, /device:TPU:8, one launch (start us, length us, event | category | flops | bytes accessed | tf_op | source)
XLA Modules:
  0.0 1378.4 jit_solution(10861475274174279404)
XLA Ops:
  17.2 478.5 %while.16 = (s32[]{:T(128)}, f32[6,6,8,512]{3,0,1,2:T(8,128)S(1)}, f32[2,2,2,6,512]{4,3,2,1,0:T(8,128)S(1)}, f32[8,10,512]{2,0,1:T(8,128)S(1)}, f32[8,10,512]{2,...) while((s32[]{:T(128)}, f32[6,6,8,512]{3,0,1,2:T(8,128)S(1)}, ...), condition=%wide.region_1.2_spmd.clone, body=%wide.region_0.1_spmd.clone.sunk | while | flops 2527413 | bytes 23437268 | solution.py:160
  21.4 8.1 collective-permute-done.1
  45.5 7.6 collective-permute-start
  72.9 12.7 collective-permute-start
  104.6 8.2 collective-permute-start
  118.4 7.1 collective-permute-start.3
  134.5 8.2 collective-permute-start
  148.3 6.9 collective-permute-start.3
  164.3 8.0 collective-permute-start
  192.8 8.9 collective-permute-start
  223.1 8.6 collective-permute-start
  252.5 9.4 collective-permute-start
  267.4 7.0 collective-permute-start.3
  283.5 10.1 collective-permute-start
  315.1 10.7 collective-permute-start
  346.2 8.2 collective-permute-start
  375.4 8.7 collective-permute-start
  405.5 8.9 collective-permute-start
  420.1 7.4 collective-permute-start.3
  436.5 8.6 collective-permute-start
  450.7 6.9 collective-permute-start.3
  466.7 10.0 collective-permute-start
  497.7 143.1 %all-reduce.18.cloned.1.call-done = f32[2,2,2,6,512]{4,3,1,0,2:T(8,128)} async-done(((f32[2,2,2,6,512]{4,3,1,0,2:T(8,128)}), f32[2,2,2,6,512]{4,3,1,0,2:T(8,128)}) %all-reduce.18.cloned.1.call-update) | async-done | bytes 98320 | tf_op jit(solution)/shard_map/psum | solution.py:30
  653.4 716.9 %all-reduce.20.cloned.1.call-done = f32[384,2,2,2,64]{4,3,2,1,0:T(2,128)} async-done(((f32[384,2,2,2,64]{4,3,2,1,0:T(2,128)}), f32[384,2,2,2,64]{4,3,2,1,0:T(2,128)}) %all-reduce.20.cloned.1.call-update) | async-done | bytes 786448
  (691 shorter events, 311.6 us)
Async XLA Ops:
  7.2 633.7 %all-reduce.18.cloned.1.call-start = ((), (), s32[]{:S(2)}) async-start(), calls=%async_computation | async-start | bytes 262144 | tf_op jit(solution)/shard_map/psum | solution.py:30
  19.3 10.2 collective-permute-start.1
  72.9 14.4 %collective-permute-start = (f32[6,6,1,512]{3,1,2,0:T(8,128)S(1)}, f32[6,6,1,512]{3,1,2,0:T(8,128)S(1)}, u32[]{:S(2)}, u32[]{:S(2)}) collective-permute-start(f32[6,6,1,512]{3,1,2,0:T(8,128)S(1)} %get-tuple-element.301), channel_id=1, source_target_pairs={{0,64},{64,128},{128,192},{192,256},{256,320},{320,384},{384,448},... | collective-permute-start | bytes 221192 | tf_op jit(solution)/shard_map/while/body/eval_jaxpr/ppermute | solution.py:20
  104.6 9.9 collective-permute-start
  116.4 10.0 collective-permute-start.2
  134.5 9.9 collective-permute-start
  146.4 9.8 collective-permute-start.2
  164.3 9.7 collective-permute-start
  192.8 10.6 collective-permute-start
  223.1 10.3 collective-permute-start
  252.5 11.1 collective-permute-start
  265.5 9.9 collective-permute-start.2
  283.5 11.8 collective-permute-start
  315.1 12.4 collective-permute-start
  346.2 9.9 collective-permute-start
  375.4 10.4 collective-permute-start
  387.8 9.6 collective-permute-start.2
  405.5 10.6 collective-permute-start
  418.1 10.3 collective-permute-start.2
  420.1 9.9 collective-permute-start.3
  436.5 10.3 collective-permute-start
  448.8 9.8 collective-permute-start.2
  466.7 11.7 collective-permute-start
  496.4 873.9 %all-reduce.20.cloned.1.call-start = ((), (), s32[]{:S(2)}) async-start(), calls=%async_computation.1 | async-start | bytes 3145728
  (61 other events, 296.6 us)
Sparse Core Ops, SparseCore 0:
  496.5 144.3 all-reduce.17
  650.4 719.8 all-reduce.19
where the time goes:
time: 1380 us
  waiting for transfers between devices  924 us (67%)
  starting transfers between devices  287 us (21%)
  local copies, waits for them, and re-layouts  81.5 us (6%)
  other arithmetic  52.3 us (4%)
  between operations  14.9 us (1%)
    unnamed x3, waiting for transfers between devices  717 us
    ppermute x32, starting transfers between devices, padded_2(): lax.ppermute(lax.slice_in_dim(block, block.shape[dim] - width, None, axis...  235 us
    psum x1, waiting for transfers between devices, from_root(): return lax.psum(block, axis)  143 us
    ppermute x32, starting transfers between devices, padded_2(): lax.ppermute(lax.slice_in_dim(block, 0, width, axis=dim), axis, backward)  51.8 us
    another operation x112, local copies, waits for them, and re-layouts, yee_step(): return jnp.stack([new_x, new_y, new_z, magn_x, magn_y, magn_z])  40.2 us
    ppermute x32, waiting for transfers between devices, padded_2(): lax.ppermute(lax.slice_in_dim(block, 0, width, axis=dim), axis, backward)  38.8 us
  transfers between devices with their start and end apart: 66, of which 50 were waited for; matrix products, arithmetic and copies ran while one was open for 1% of the time, Pallas kernels for 0%

commit v1 on v0

--- a/solution.py
+++ b/solution.py
@@ -10,6 +10,11 @@
 SOURCE_AMP = 1.0
 QUARTERS = (3, 5)
 HIGHEST = lax.Precision.HIGHEST
+
+
+def wait_face(shard_axis, here_x):
+    newest = jnp.sum(jax.lax.all_gather(here_x, shard_axis), axis=0)
+    return newest
 
 
 def padded_2(block, sides, width):
@@ -27,7 +32,7 @@
 
 def from_root(block, axis, owner):
     block = jnp.where(lax.axis_index(axis) == owner, block, jnp.zeros_like(block))
-    return lax.psum(block, axis)
+    return wait_face(axis, here_x=block)
 
 
 def forward_diff(field, along):

time: 1380 us -> 1310 us (0.949)
  waiting for transfers between devices: 924 us -> 824 us
  blocking collectives: 0 us -> 30.8 us
    psum x1 -> x0, waiting for transfers between devices: 143 us -> none  [from_root(): return lax.psum(block, axis)]
    unnamed x3 -> x2, waiting for transfers between devices: 717 us -> 759 us
    all_gather x0 -> x1, blocking collectives: none -> 30.8 us  [wait_face(): newest = jnp.sum(jax.lax.all_gather(here_x, shard_axis), axis=0)]
  transfers between devices with their start and end apart: 66 -> 65, of which waited for: 50 -> 49; matrix products, arithmetic and copies ran while one was open for 1% -> 1% of each run, Pallas kernels for 0% -> 0%
where the time goes in v1:
time: 1310 us
  waiting for transfers between devices  824 us (63%)
  starting transfers between devices  287 us (22%)
  local copies, waits for them, and re-layouts  81.6 us (6%)
  other arithmetic  53.1 us (4%)
  blocking collectives  30.8 us (2%)
  between operations  14.9 us (1%)
    unnamed x2, waiting for transfers between devices  759 us
    ppermute x32, starting transfers between devices, padded_2(): lax.ppermute(lax.slice_in_dim(block, block.shape[dim] - width, None, axis...  235 us
    ppermute x32, starting transfers between devices, padded_2(): lax.ppermute(lax.slice_in_dim(block, 0, width, axis=dim), axis, backward)  51.8 us
    another operation x112, local copies, waits for them, and re-layouts, yee_step(): return jnp.stack([new_x, new_y, new_z, magn_x, magn_y, magn_z])  40.2 us
    ppermute x32, waiting for transfers between devices, padded_2(): lax.ppermute(lax.slice_in_dim(block, 0, width, axis=dim), axis, backward)  38.7 us
    all_gather x1, blocking collectives, wait_face(): newest = jnp.sum(jax.lax.all_gather(here_x, shard_axis), axis=0)  30.8 us
  transfers between devices with their start and end apart: 65, of which 49 were waited for; matrix products, arithmetic and copies ran while one was open for 1% of the time, Pallas kernels for 0%

profile of v1, /device:TPU:8, one launch (start us, length us, event | category | flops | bytes accessed | tf_op | source)
XLA Modules:
  0.0 1306.0 jit_solution(12515792505660795563)
XLA Ops:
  19.2 478.5 %while.16 = (s32[]{:T(128)}, f32[6,6,8,512]{3,0,1,2:T(8,128)S(1)}, f32[2,2,2,6,512]{4,3,2,1,0:T(8,128)S(1)}, f32[8,10,512]{2,0,1:T(8,128)S(1)}, f32[8,10,512]{2,...) while((s32[]{:T(128)}, f32[6,6,8,512]{3,0,1,2:T(8,128)S(1)}, ...), condition=%wide.region_1.2_spmd.clone, body=%wide.region_0.1_spmd.clone.sunk | while | flops 2527413 | bytes 23437268 | solution.py:165
  23.4 8.1 collective-permute-done.1
  47.5 7.6 collective-permute-start
  74.9 12.7 collective-permute-start
  106.6 8.2 collective-permute-start
  120.4 7.1 collective-permute-start.3
  136.6 8.2 collective-permute-start
  150.4 6.9 collective-permute-start.3
  166.4 8.0 collective-permute-start
  194.9 8.9 collective-permute-start
  225.2 8.6 collective-permute-start
  254.5 9.4 collective-permute-start
  269.5 7.0 collective-permute-start.3
  285.6 10.1 collective-permute-start
  317.2 10.7 collective-permute-start
  348.3 8.2 collective-permute-start
  362.1 9.4 collective-permute-start.3
  380.6 8.7 collective-permute-start
  409.8 8.2 collective-permute-start
  423.6 7.2 collective-permute-start.3
  439.8 8.4 collective-permute-start
  468.7 9.0 collective-permute-start
  497.9 30.8 %all-gather = f32[16,2,2,6,512]{4,2,3,1,0:T(2,128)S(1)} all-gather(f32[2,2,2,6,512]{4,2,3,1,0:T(2,128)S(1)} %copy_select_fusion), channel_id=2, replica_groups=mesh['depth'=8,'lat'=64] {'depth'}, dimensions={0}, use_global_device_ids=true | all-gather | bytes 884736 | tf_op jit(solution)/shard_map/all_gather | solution.py:16
  538.5 759.4 %all-reduce.17.cloned.1.call-done = f32[384,2,2,2,64]{4,3,2,1,0:T(2,128)} async-done(((f32[384,2,2,2,64]{4,3,2,1,0:T(2,128)}), f32[384,2,2,2,64]{4,3,2,1,0:T(2,128)}) %all-reduce.17.cloned.1.call-update) | async-done | bytes 786448
  (699 shorter events, 308.5 us)
Async XLA Ops:
  7.2 1290.6 %all-reduce.17.cloned.1.call-start = ((), (), s32[]{:S(2)}) async-start(), calls=%async_computation | async-start | bytes 3145728
  21.3 10.2 collective-permute-start.1
  74.9 14.4 %collective-permute-start = (f32[6,6,1,512]{3,1,2,0:T(8,128)S(1)}, f32[6,6,1,512]{3,1,2,0:T(8,128)S(1)}, u32[]{:S(2)}, u32[]{:S(2)}) collective-permute-start(f32[6,6,1,512]{3,1,2,0:T(8,128)S(1)} %get-tuple-element.303), channel_id=1, source_target_pairs={{0,64},{64,128},{128,192},{192,256},{256,320},{320,384},{384,448},... | collective-permute-start | bytes 221192 | tf_op jit(solution)/shard_map/while/body/eval_jaxpr/ppermute | solution.py:25
  106.6 9.9 collective-permute-start
  118.5 10.0 collective-permute-start.2
  136.6 9.9 collective-permute-start
  148.5 9.8 collective-permute-start.2
  166.4 9.7 collective-permute-start
  194.9 10.6 collective-permute-start
  207.5 9.6 collective-permute-start.2
  225.2 10.3 collective-permute-start
  254.5 11.1 collective-permute-start
  267.6 9.9 collective-permute-start.2
  285.6 11.8 collective-permute-start
  317.2 12.4 collective-permute-start
  348.3 9.9 collective-permute-start
  360.2 12.3 collective-permute-start.2
  362.1 11.9 collective-permute-start.3
  380.6 10.4 collective-permute-start
  409.8 9.9 collective-permute-start
  421.7 10.0 collective-permute-start.2
  423.6 9.6 collective-permute-start.3
  439.8 10.1 collective-permute-start
  468.7 10.7 collective-permute-start
  (64 other events, 413.2 us)
Sparse Core Ops, SparseCore 0:
  535.5 762.2 all-reduce.16
